TPU v7x, 256 devices: a whole 4x4x8 slice. The times are simulated.
256 devices in a mesh: exp: 64 (over z, y, core), voc: 4 (over x).
Axes of the slice: x: 4, y: 4, z: 8, core: 2. Of those that a mesh axis runs over, the one named last changes fastest.
Arguments:
- tokens: bfloat16 [2048, 4096], P('exp', 'voc'), may hold values from -6 to 6
- expert_routes: int32 [2048, 2], P('exp'), may hold values from 0 to 7, all different within a row; in each aligned block of 32 rows (0 to 31, 32 to 63, ...) at most 16 rows name the same one
- gate_scores: float32 [2048, 2], P('exp'), may hold values from 0.2 to 1
- w_gate: bfloat16 [64, 4096, 1792], P('exp', None, 'voc'), may hold values from -0.09375 to 0.09375
- w_up: bfloat16 [64, 4096, 1792], P('exp', None, 'voc'), may hold values from -0.09375 to 0.09375
- w_down: bfloat16 [64, 1792, 4096], P('exp', 'voc'), may hold values from -0.046875 to 0.046875
- head_weight: bfloat16 [4096, 32000], P('voc', 'exp'), may hold values from -0.09375 to 0.09375
- passage_ids: int32 [64, 32], replicated, may hold values from 0 to 3, never falling along the last dimension, each value on 1 to 16 neighbouring positions
- doc_length: int32 [64, 4], replicated, may hold values from 20 to 180, as said below
Outputs:
- term_scores: float32 [256, 32000], P('voc', 'exp')
Inputs may be any that keep to these rules, and one draw needn't show every extreme that they name: `expert_routes`: each row names 2 different experts; among the rows of one exp index (32 tokens) no expert is named more than 16 times. `passage_ids`: never falling along a row; every passage holds 1 to 16 tokens. `doc_length`: positive whole numbers of words.
All inputs are finite; a program needn't handle non-finite values.
Results may differ from a plain program's by a relative error of at most 0.0065.
Values may be sent and summed in bfloat16 or wider, within the bound.
A program may use at most 128 MiB of HBM per device.

v0:
```python
import jax
import jax.numpy as jnp
from jax import lax
from jax.sharding import PartitionSpec as P

EXPERTS = 8


def slot_tables(route_rows, gate_rows, capacity):
    count = route_rows.shape[0]
    expert_ids = jnp.arange(EXPERTS, dtype=jnp.int32)
    hit_table = (route_rows[:, :, None] == expert_ids).astype(jnp.int32)
    flat_hits = hit_table.reshape(count * 2, EXPERTS)
    rank_table = jnp.cumsum(flat_hits, axis=0) - flat_hits
    slot_table = jnp.sum(flat_hits * rank_table, axis=1).reshape(count, 2)
    slot_ids = jnp.arange(capacity, dtype=jnp.int32)
    matches = hit_table[:, :, :, None] * (slot_table[:, :, None, None] == slot_ids).astype(
        jnp.int32
    )
    place_table = jnp.sum(matches, axis=1)
    gate_table = jnp.sum(matches.astype(jnp.float32) * gate_rows[:, :, None, None], axis=1)
    return (place_table, gate_table)


def build_slots(place_table, token_rows, group_size):
    slot_rows = jnp.einsum(
        "tec,td->ecd",
        place_table.astype(jnp.bfloat16),
        token_rows,
        preferred_element_type=jnp.float32,
    ).astype(jnp.bfloat16)
    return jnp.repeat(slot_rows, group_size, axis=0)


def local(
    tokens, expert_routes, gate_scores, w_gate, w_up, w_down, head_weight, passage_ids, doc_length
):
    tok_count, width_slice = tokens.shape
    capacity = tok_count // 2
    exp_count = lax.axis_size("exp")
    voc_count = lax.axis_size("voc")
    group_size = exp_count // EXPERTS
    place_table, gate_table = slot_tables(expert_routes, gate_scores, capacity)
    gate_local = w_gate[0]
    up_local = w_up[0]
    down_local = w_down[0]
    slot_count = exp_count * capacity
    send_rows = build_slots(place_table, tokens, group_size)
    received = lax.all_to_all(send_rows, "exp", split_axis=0, concat_axis=0, tiled=True)
    received = received.reshape(slot_count, width_slice)
    block_rows = lax.all_gather(received, "voc", axis=1, tiled=True)
    gate_pre = jnp.dot(block_rows, gate_local, preferred_element_type=jnp.float32)
    up_pre = jnp.dot(block_rows, up_local, preferred_element_type=jnp.float32)
    hidden = (jax.nn.silu(gate_pre) * up_pre).astype(jnp.bfloat16)
    part = jnp.dot(hidden, down_local, preferred_element_type=jnp.float32)
    rounded = lax.optimization_barrier(part.astype(jnp.bfloat16)).astype(jnp.float32)
    rounded = rounded.reshape(exp_count, capacity, rounded.shape[1])
    summed = lax.psum_scatter(rounded.astype(jnp.bfloat16), "voc", scatter_dimension=2, tiled=True)
    returned = lax.all_to_all(summed, "exp", split_axis=0, concat_axis=0, tiled=True)
    member_sum = jnp.sum(
        returned.astype(jnp.float32).reshape(EXPERTS, group_size, capacity, width_slice), axis=1
    )
    moe = jnp.einsum("tec,ecd->td", gate_table, member_sum, precision=lax.Precision.HIGHEST)
    layer_out = (tokens.astype(jnp.float32) + moe).astype(jnp.bfloat16)
    gathered = lax.all_gather(layer_out, "exp", axis=0, tiled=True)
    logits = lax.psum_scatter(
        jnp.dot(gathered, head_weight, preferred_element_type=jnp.float32).astype(jnp.bfloat16),
        "voc",
        scatter_dimension=0,
        tiled=True,
    ).astype(jnp.float32)
    saturated = jnp.log1p(jnp.maximum(logits, 0.0))
    shards_here = exp_count // voc_count
    pass_count = doc_length.shape[1]
    first_shard = lax.axis_index("voc") * shards_here
    ids_here = lax.dynamic_slice_in_dim(passage_ids, first_shard, shards_here, 0)
    lengths_here = lax.dynamic_slice_in_dim(doc_length, first_shard, shards_here, 0)
    one_hot = (
        ids_here[:, None, :] == jnp.arange(pass_count, dtype=jnp.int32)[None, :, None]
    ).astype(jnp.float32)
    saturated = saturated.reshape(shards_here, tok_count, saturated.shape[1])
    freq = jnp.einsum("spt,stv->spv", one_hot, saturated, precision=lax.Precision.HIGHEST)
    avg_length = jnp.sum(doc_length.astype(jnp.float32)) / (doc_length.shape[0] * pass_count)
    scale = 1.0 - 0.75 + 0.75 * lengths_here.astype(jnp.float32) / avg_length
    scores = freq * (1.2 + 1.0) / (freq + 1.2 * scale[:, :, None])
    return scores.reshape(shards_here * pass_count, scores.shape[2])


def solution(mesh):
    in_specs = (
        P("exp", "voc"),
        P("exp", None),
        P("exp", None),
        P("exp", None, "voc"),
        P("exp", None, "voc"),
        P("exp", "voc", None),
        P("voc", "exp"),
        P(),
        P(),
    )
    out_specs = P("voc", "exp")
    return jax.shard_map(local, mesh=mesh, in_specs=in_specs, out_specs=out_specs, check_vma=False)
```

profile of v0, /device:TPU:1, one launch (start us, length us, event | category | flops | bytes accessed | tf_op | source)
XLA Modules:
  0.0 445.1 jit_solution(3002805824108448492)
XLA Ops:
  6.5 0.8 copy.23
  7.4 0.7 fusion.20
  8.1 0.1 eq.65
  8.2 0.1 fusion.16
  8.2 0.1 reduce_window_sum.11
  8.3 0.2 select_reduce_fusion
  8.5 0.1 eq.69
  8.6 0.1 copy.24
  8.8 1.0 convolution_convert_fusion.2
  9.8 0.3 broadcast_in_dim.2
  10.1 62.7 %all_to_all.10 = bf16[64,16,1024]{2,1,0:T(8,128)(2,1)} all-to-all(bf16[64,16,1024]{2,1,0:T(8,128)(2,1)S(1)} %bitcast.38), channel_id=1, replica_groups=mesh['exp'=64,'voc'=4] {'exp'}, dimensions={0} | all-to-all | bytes 4194304 | tf_op jit(solution)/shard_map/all_to_all | solution.py:49
  72.9 83.4 %all-gather.3.cloned.1.call-done = bf16[1024,4096]{1,0:T(8,128)(2,1)} async-done(((bf16[1024,1024]{1,0:T(8,128)(2,1)}), bf16[1024,4096]{1,0:T(8,128)(2,1)}) %all-gather.3.cloned.1.call-update) | async-done | bytes 8388624 | tf_op jit(solution)/shard_map/all_gather | solution.py:51
  156.3 7.5 %fusion.3 = f32[1024,448]{0,1:T(8,128)S(1)} fusion(bf16[1024,4096]{1,0:T(8,128)(2,1)} %all-gather.3.cloned.1.call-done, bf16[1,4096,448]{1,2,0:T(8,128)(2,1)} %param.12), kind=kOutput, calls=%fused_computation.5 | convolution fusion | flops 3758096384 | bytes 13893632 | tf_op jit(solution)/shard_map/dot_general | solution.py:52
  163.8 15.2 %convolution_convert_fusion = bf16[1024,4096]{1,0:T(8,128)(2,1)} fusion(bf16[1,448,4096]{2,1,0:T(8,128)(2,1)} %param.14, f32[1024,448]{0,1:T(8,128)S(1)} %fusion.3, bf16[1024,4096]{1,0:T(8,128)(2,1)} %all-gather.3.cloned.1.call-done, bf16[1,4096,448]{1,2,0:T(8,128)(2,1)} %param.13), kind=kOutput, calls=%fused_computation | convolution fusion | flops 7523139584 | bytes 25952256 | tf_op jit(solution)/shard_map/dot_general | solution.py:55
  179.1 84.3 %reduce-scatter.3.cloned.1.call-done = bf16[64,16,1024]{2,1,0:T(8,128)(2,1)} async-done(((bf16[64,16,4096]{2,1,0:T(8,128)(2,1)}), bf16[64,16,1024]{2,1,0:T(8,128)(2,1)}) %reduce-scatter.3.cloned.1.call-update) | async-done | bytes 2097168 | tf_op jit(solution)/shard_map/reduce_scatter | solution.py:58
  263.4 10.6 %all-to-all-start.1 = ((bf16[64,16,1024]{2,1,0:T(8,128)(2,1)}), bf16[64,16,1024]{2,1,0:T(8,128)(2,1)S(1)}, u32[]{:S(2)}, u32[]{:S(2)}) async-start(bf16[64,16,1024]{2,1,0:T(8,128)(2,1)} %reduce-scatter.3.cloned.1.call-done), calls=%async_computation.2 | async-start | bytes 4194304 | tf_op jit(solution)/shard_map/all_to_all | solution.py:59
  274.1 49.6 %all-to-all-done.1 = bf16[64,16,1024]{2,1,0:T(8,128)(2,1)S(1)} async-done(((bf16[64,16,1024]{2,1,0:T(8,128)(2,1)}), bf16[64,16,1024]{2,1,0:T(8,128)(2,1)S(1)}, u32[]{:S(2)}, u32[]{:S(2)}) %all-to-all-start.1) | async-done | bytes 2097184 | tf_op jit(solution)/shard_map/all_to_all | solution.py:59
  323.7 0.4 convert_reduce_fusion
  324.0 1.0 fusion.10
  325.1 0.2 reduce-scatter.5.cloned.1.call-start
  325.4 75.4 %all-gather.5.cloned.1.call-done = bf16[2048,1024]{1,0:T(8,128)(2,1)} async-done(((bf16[32,1024]{1,0:T(8,128)(2,1)}), bf16[2048,1024]{1,0:T(8,128)(2,1)}) %all-gather.5.cloned.1.call-update) | async-done | bytes 4194320 | tf_op jit(solution)/shard_map/all_gather | solution.py:65
  400.8 5.8 %convolution_convert_fusion.1 = bf16[2048,500]{0,1:T(8,128)(2,1)} fusion(bf16[2048,1024]{1,0:T(8,128)(2,1)} %all-gather.5.cloned.1.call-done, bf16[1024,500]{0,1:T(8,128)(2,1)S(1)} %copy-done), kind=kOutput, calls=%fused_computation.7 | convolution fusion | flops 2098176000 | bytes 7266304 | tf_op jit(solution)/shard_map/dot_general | solution.py:67
  406.7 0.1 constant_dynamic-slice_fusion
  406.7 0.1 copy.22
  406.8 0.6 convert_reduce_fusion.1
  408.1 0.1 add_multiply_fusion
  408.2 0.1 copy.26
  408.2 27.4 %reduce-scatter.5.cloned.1.call-done = bf16[512,500]{0,1:T(8,128)(2,1)} async-done(((bf16[2048,500]{0,1:T(8,128)(2,1)}), bf16[512,500]{0,1:T(8,128)(2,1)}) %reduce-scatter.5.cloned.1.call-update) | async-done | bytes 512016 | tf_op jit(solution)/shard_map/reduce_scatter | solution.py:66
  435.6 1.4 maximum_log-plus-one_fusion
  437.1 0.3 copy.25
  437.4 0.5 add_divide_fusion
  437.9 0.7 reshape.46
  (20 shorter events, 0.2 us)
Async XLA Ops:
  6.5 394.3 %copy-start = (bf16[1024,500]{0,1:T(8,128)(2,1)S(1)}, bf16[1024,500]{0,1:T(8,128)(2,1)}, u32[]{:S(2)}) copy-start(bf16[1024,500]{0,1:T(8,128)(2,1)} %param.15) | copy-start | bytes 3072004
  6.5 149.7 %all-gather.3.cloned.1.call-start = ((), (), s32[]{:S(2)}) async-start(), calls=%async_computation.4 | async-start | bytes 10485760 | tf_op jit(solution)/shard_map/all_gather | solution.py:51
  72.8 190.5 %reduce-scatter.3.cloned.1.call-start = ((), (), s32[]{:S(2)}) async-start(), calls=%async_computation.5 | async-start | bytes 10485760 | tf_op jit(solution)/shard_map/reduce_scatter | solution.py:58
  179.1 95.0 %copy-start.4 = (f32[32,2]{0,1:T(2,128)S(1)}, f32[32,2]{0,1:T(2,128)}, u32[]{:S(2)}) copy-start(f32[32,2]{0,1:T(2,128)} %param.11) | copy-start | bytes 772
  179.1 144.9 %copy-start.1 = (bf16[32,1024]{1,0:T(8,128)(2,1)S(1)}, bf16[32,1024]{1,0:T(8,128)(2,1)}, u32[]{:S(2)}) copy-start(bf16[32,1024]{1,0:T(8,128)(2,1)} %param.9) | copy-start | bytes 196612
  263.4 60.3 %all-to-all-start.1 = ((bf16[64,16,1024]{2,1,0:T(8,128)(2,1)}), bf16[64,16,1024]{2,1,0:T(8,128)(2,1)S(1)}, u32[]{:S(2)}, u32[]{:S(2)}) async-start(bf16[64,16,1024]{2,1,0:T(8,128)(2,1)} %reduce-scatter.3.cloned.1.call-done), calls=%async_computation.2 | async-start | bytes 4194304 | tf_op jit(solution)/shard_map/all_to_all | solution.py:59
  274.0 126.8 %all-gather.5.cloned.1.call-start = ((), (), s32[]{:S(2)}) async-start(), calls=%async_computation.6 | async-start | bytes 4259840 | tf_op jit(solution)/shard_map/all_gather | solution.py:65
  325.1 81.6 %copy-start.2 = (s32[64,32]{0,1:T(8,128)S(1)}, s32[64,32]{0,1:T(8,128)}, u32[]{:S(2)}) copy-start(s32[64,32]{0,1:T(8,128)} %param.16) | copy-start | bytes 24580
  325.1 81.7 %copy-start.3 = (s32[64,4]{0,1:T(4,128)S(1)}, s32[64,4]{0,1:T(4,128)}, u32[]{:S(2)}) copy-start(s32[64,4]{0,1:T(4,128)} %param.17) | copy-start | bytes 3076
  325.1 110.5 %reduce-scatter.5.cloned.1.call-start = ((), (), s32[]{:S(2)}) async-start(), calls=%async_computation.7 | async-start | bytes 2580480 | tf_op jit(solution)/shard_map/reduce_scatter | solution.py:66
Sparse Core Ops, SparseCore 0:
  73.0 83.2 all-gather.2
  179.2 84.1 reduce-scatter.2
  325.2 75.5 all-gather.4
  406.8 28.8 reduce-scatter.4
where the time goes:
time: 445 us
  waiting for transfers between devices  320 us (72%)
  blocking collectives  62.7 us (14%)
  matrix products  31.2 us (7%)
  between operations  13.9 us (3%)
  starting transfers between devices  10.9 us (2%)
    reduce_scatter x1, waiting for transfers between devices, local(): lax.psum_scatter(rounded.astype(jnp.bfloat16), 'voc', scatter_dimension=2...  84.3 us
    all_gather x1, waiting for transfers between devices, local(): block_rows = lax.all_gather(received, 'voc', axis=1, tiled=True)  83.4 us
    all_gather x1, waiting for transfers between devices, local(): gathered = lax.all_gather(layer_out, 'exp', axis=0, tiled=True)  75.4 us
    all_to_all x1, blocking collectives, local(): lax.all_to_all(send_rows, 'exp', split_axis=0, concat_axis=0, tiled=True)  62.7 us
    all_to_all x1, waiting for transfers between devices, local(): lax.all_to_all(summed, 'exp', split_axis=0, concat_axis=0, tiled=True)  49.6 us
    reduce_scatter x1, waiting for transfers between devices, local(): lax.psum_scatter(jnp.dot(gathered, head_weight, preferred_element_type=jn...  27.4 us
    dot_general x1, matrix products, local(): part = jnp.dot(hidden, down_local, preferred_element_type=jnp.float32)  15.2 us
    all_to_all x1, starting transfers between devices, local(): lax.all_to_all(summed, 'exp', split_axis=0, concat_axis=0, tiled=True)  10.6 us
  transfers between devices with their start and end apart: 5, of which 5 were waited for; matrix products, arithmetic and copies ran while one was open for 0% of the time, Pallas kernels for 0%

commit v1 on v0

--- a/solution.py
+++ b/solution.py
@@ -48,7 +48,9 @@
     send_rows = build_slots(place_table, tokens, group_size)
     received = lax.all_to_all(send_rows, "exp", split_axis=0, concat_axis=0, tiled=True)
     received = received.reshape(slot_count, width_slice)
-    block_rows = lax.all_gather(received, "voc", axis=1, tiled=True)
+    block_rows = jnp.concatenate(
+        lax.all_to_all(jnp.stack([received] * lax.axis_size("voc")), "voc", 0, 0), axis=1
+    )
     gate_pre = jnp.dot(block_rows, gate_local, preferred_element_type=jnp.float32)
     up_pre = jnp.dot(block_rows, up_local, preferred_element_type=jnp.float32)
     hidden = (jax.nn.silu(gate_pre) * up_pre).astype(jnp.bfloat16)

time: 445 us -> 460 us (1.034)
  blocking collectives: 62.7 us -> 158 us
  waiting for transfers between devices: 320 us -> 234 us
  local copies, waits for them, and re-layouts: 2.67 us -> 9.94 us
    all_to_all x0 -> x1, blocking collectives: none -> 95.4 us  [local(): lax.all_to_all(jnp.stack([received] * lax.axis_size('voc')), 'voc', 0, 0)]
    all_gather x1 -> x0, waiting for transfers between devices: 83.4 us -> none  [local(): block_rows = lax.all_gather(received, 'voc', axis=1, tiled=True)]
  transfers between devices with their start and end apart: 5 -> 4, of which waited for: 5 -> 4; matrix products, arithmetic and copies ran while one was open for 0% -> 0% of each run, Pallas kernels for 0% -> 0%
where the time goes in v1:
time: 460 us
  waiting for transfers between devices  234 us (51%)
  blocking collectives  158 us (34%)
  matrix products  29 us (6%)
  between operations  13.9 us (3%)
  starting transfers between devices  10.9 us (2%)
  local copies, waits for them, and re-layouts  9.94 us (2%)
    all_to_all x1, blocking collectives, local(): lax.all_to_all(jnp.stack([received] * lax.axis_size('voc')), 'voc', 0, 0)  95.4 us
    reduce_scatter x1, waiting for transfers between devices, local(): lax.psum_scatter(rounded.astype(jnp.bfloat16), 'voc', scatter_dimension=2...  81.7 us
    all_gather x1, waiting for transfers between devices, local(): gathered = lax.all_gather(layer_out, 'exp', axis=0, tiled=True)  75.4 us
    all_to_all x1, blocking collectives, local(): lax.all_to_all(send_rows, 'exp', split_axis=0, concat_axis=0, tiled=True)  62.7 us
    all_to_all x1, waiting for transfers between devices, local(): lax.all_to_all(summed, 'exp', split_axis=0, concat_axis=0, tiled=True)  49.6 us
    reduce_scatter x1, waiting for transfers between devices, local(): lax.psum_scatter(jnp.dot(gathered, head_weight, preferred_element_type=jn...  27.4 us
    dot_general x1, matrix products, local(): part = jnp.dot(hidden, down_local, preferred_element_type=jnp.float32)  15.4 us
    all_to_all x1, starting transfers between devices, local(): lax.all_to_all(summed, 'exp', split_axis=0, concat_axis=0, tiled=True)  10.6 us
  transfers between devices with their start and end apart: 4, of which 4 were waited for; matrix products, arithmetic and copies ran while one was open for 0% of the time, Pallas kernels for 0%

profile of v1, /device:TPU:1, one launch (start us, length us, event | category | flops | bytes accessed | tf_op | source)
XLA Modules:
  0.0 459.6 jit_solution(15644424020593487010)
XLA Ops:
  6.5 0.8 copy.31
  7.4 0.7 fusion.20
  8.1 0.1 eq.65
  8.2 0.1 reduce_window_sum.11
  8.3 0.2 select_reduce_fusion
  8.5 0.1 eq.69
  8.8 1.0 convolution_convert_fusion.2
  9.8 0.3 broadcast_in_dim.2
  10.1 62.7 %all_to_all.15 = bf16[64,16,1024]{2,1,0:T(8,128)(2,1)} all-to-all(bf16[64,16,1024]{2,1,0:T(8,128)(2,1)S(1)} %bitcast.42), channel_id=1, replica_groups=mesh['exp'=64,'voc'=4] {'exp'}, dimensions={0} | all-to-all | bytes 4194304 | tf_op jit(solution)/shard_map/all_to_all | solution.py:49
  72.8 2.9 copy.33
  75.7 1.2 stack.3
  76.9 95.4 %all_to_all.16 = bf16[4,1024,1024]{1,2,0:T(8,128)(2,1)S(1)} all-to-all(bf16[4,1024,1024]{1,2,0:T(8,128)(2,1)S(1)} %stack.3), channel_id=1, replica_groups=mesh['exp'=64,'voc'=4] {'voc'}, dimensions={0} | all-to-all | bytes 16777216 | tf_op jit(solution)/shard_map/all_to_all | solution.py:52
  172.3 3.2 copy-done.1
  175.5 5.2 %fusion.3 = f32[1024,448]{0,1:T(8,128)} fusion(bf16[1024,4096]{0,1:T(8,128)(2,1)S(1)} %bitcast.40, bf16[1,4096,448]{1,2,0:T(8,128)(2,1)S(1)} %copy-done.6), kind=kOutput, calls=%fused_computation.5 | convolution fusion | flops 3758096384 | bytes 13893632 | tf_op jit(solution)/shard_map/dot_general | solution.py:54
  180.7 15.4 %convolution_convert_fusion = bf16[1024,4096]{1,0:T(8,128)(2,1)} fusion(bf16[1,448,4096]{2,1,0:T(8,128)(2,1)} %param.14, f32[1024,448]{0,1:T(8,128)} %fusion.3, bf16[1024,4096]{0,1:T(8,128)(2,1)} %bitcast.41, bf16[1,4096,448]{1,2,0:T(8,128)(2,1)} %param.13), kind=kOutput, calls=%fused_computation | convolution fusion | flops 7523139584 | bytes 25952256 | tf_op jit(solution)/shard_map/dot_general | solution.py:57
  196.2 81.7 %reduce-scatter.3.cloned.1.call-done = bf16[64,16,1024]{2,1,0:T(8,128)(2,1)} async-done(((bf16[64,16,4096]{2,1,0:T(8,128)(2,1)}), bf16[64,16,1024]{2,1,0:T(8,128)(2,1)}) %reduce-scatter.3.cloned.1.call-update) | async-done | bytes 2097168 | tf_op jit(solution)/shard_map/reduce_scatter | solution.py:60
  277.9 10.6 %all-to-all-start.2 = ((bf16[64,16,1024]{2,1,0:T(8,128)(2,1)}), bf16[64,16,1024]{2,1,0:T(8,128)(2,1)S(1)}, u32[]{:S(2)}, u32[]{:S(2)}) async-start(bf16[64,16,1024]{2,1,0:T(8,128)(2,1)} %reduce-scatter.3.cloned.1.call-done), calls=%async_computation.3 | async-start | bytes 4194304 | tf_op jit(solution)/shard_map/all_to_all | solution.py:61
  288.6 49.6 %all-to-all-done.2 = bf16[64,16,1024]{2,1,0:T(8,128)(2,1)S(1)} async-done(((bf16[64,16,1024]{2,1,0:T(8,128)(2,1)}), bf16[64,16,1024]{2,1,0:T(8,128)(2,1)S(1)}, u32[]{:S(2)}, u32[]{:S(2)}) %all-to-all-start.2) | async-done | bytes 2097184 | tf_op jit(solution)/shard_map/all_to_all | solution.py:61
  338.2 0.4 convert_reduce_fusion
  338.6 1.0 fusion.10
  339.6 0.2 reduce-scatter.5.cloned.1.call-start
  339.9 75.4 %all-gather.2.cloned.1.call-done = bf16[2048,1024]{1,0:T(8,128)(2,1)} async-done(((bf16[32,1024]{1,0:T(8,128)(2,1)}), bf16[2048,1024]{1,0:T(8,128)(2,1)}) %all-gather.2.cloned.1.call-update) | async-done | bytes 4194320 | tf_op jit(solution)/shard_map/all_gather | solution.py:67
  415.3 5.9 %convolution_convert_fusion.1 = bf16[2048,500]{0,1:T(8,128)(2,1)} fusion(bf16[2048,1024]{1,0:T(8,128)(2,1)} %all-gather.2.cloned.1.call-done, bf16[1024,500]{0,1:T(8,128)(2,1)S(1)} %copy-done), kind=kOutput, calls=%fused_computation.7 | convolution fusion | flops 2098176000 | bytes 7266304 | tf_op jit(solution)/shard_map/dot_general | solution.py:69
  421.2 0.1 constant_dynamic-slice_fusion
  421.4 0.6 convert_reduce_fusion.1
  422.6 0.1 add_multiply_fusion
  422.7 0.1 copy.35
  422.8 27.4 %reduce-scatter.5.cloned.1.call-done = bf16[512,500]{0,1:T(8,128)(2,1)} async-done(((bf16[2048,500]{0,1:T(8,128)(2,1)}), bf16[512,500]{0,1:T(8,128)(2,1)}) %reduce-scatter.5.cloned.1.call-update) | async-done | bytes 512016 | tf_op jit(solution)/shard_map/reduce_scatter | solution.py:68
  450.2 1.4 maximum_log-plus-one_fusion
  451.6 0.3 copy.34
  451.9 0.5 add_divide_fusion
  452.4 0.7 reshape.52
  (24 shorter events, 0.4 us)
Async XLA Ops:
  6.5 408.8 %copy-start = (bf16[1024,500]{0,1:T(8,128)(2,1)S(1)}, bf16[1024,500]{0,1:T(8,128)(2,1)}, u32[]{:S(2)}) copy-start(bf16[1024,500]{0,1:T(8,128)(2,1)} %param.15) | copy-start | bytes 3072004
  6.5 271.3 %reduce-scatter.3.cloned.1.call-start = ((), (), s32[]{:S(2)}) async-start(), calls=%async_computation.5 | async-start | bytes 10485760 | tf_op jit(solution)/shard_map/reduce_scatter | solution.py:60
  76.9 98.7 %copy-start.6 = (bf16[1,4096,448]{1,2,0:T(8,128)(2,1)S(1)}, bf16[1,4096,448]{1,2,0:T(8,128)(2,1)}, u32[]{:S(2)}) copy-start(bf16[1,4096,448]{1,2,0:T(8,128)(2,1)} %param.12) | copy-start | bytes 11010052
  172.3 3.2 copy-start.1
  196.2 92.4 %copy-start.5 = (f32[32,2]{0,1:T(2,128)S(1)}, f32[32,2]{0,1:T(2,128)}, u32[]{:S(2)}) copy-start(f32[32,2]{0,1:T(2,128)} %param.11) | copy-start | bytes 772
  196.2 142.4 %copy-start.2 = (bf16[32,1024]{1,0:T(8,128)(2,1)S(1)}, bf16[32,1024]{1,0:T(8,128)(2,1)}, u32[]{:S(2)}) copy-start(bf16[32,1024]{1,0:T(8,128)(2,1)} %param.9) | copy-start | bytes 196612
  277.9 60.3 %all-to-all-start.2 = ((bf16[64,16,1024]{2,1,0:T(8,128)(2,1)}), bf16[64,16,1024]{2,1,0:T(8,128)(2,1)S(1)}, u32[]{:S(2)}, u32[]{:S(2)}) async-start(bf16[64,16,1024]{2,1,0:T(8,128)(2,1)} %reduce-scatter.3.cloned.1.call-done), calls=%async_computation.3 | async-start | bytes 4194304 | tf_op jit(solution)/shard_map/all_to_all | solution.py:61
  288.5 126.8 %all-gather.2.cloned.1.call-start = ((), (), s32[]{:S(2)}) async-start(), calls=%async_computation.6 | async-start | bytes 4259840 | tf_op jit(solution)/shard_map/all_gather | solution.py:67
  339.6 81.6 %copy-start.3 = (s32[64,32]{0,1:T(8,128)S(1)}, s32[64,32]{0,1:T(8,128)}, u32[]{:S(2)}) copy-start(s32[64,32]{0,1:T(8,128)} %param.16) | copy-start | bytes 24580
  339.6 81.7 %copy-start.4 = (s32[64,4]{0,1:T(4,128)S(1)}, s32[64,4]{0,1:T(4,128)}, u32[]{:S(2)}) copy-start(s32[64,4]{0,1:T(4,128)} %param.17) | copy-start | bytes 3076
  339.6 110.5 %reduce-scatter.5.cloned.1.call-start = ((), (), s32[]{:S(2)}) async-start(), calls=%async_computation.7 | async-start | bytes 2580480 | tf_op jit(solution)/shard_map/reduce_scatter | solution.py:68
Sparse Core Ops, SparseCore 0:
  196.3 81.5 reduce-scatter.2
  339.7 75.5 all-gather.1
  421.3 28.8 reduce-scatter.4
